TPU v7x, 32 devices: a whole 2x2x4 slice. The times are simulated.
32 devices in a mesh: cfg: 2 (over x), seq: 4 (over z), tp: 4 (over y, core).
Axes of the slice: x: 2, y: 2, z: 4, core: 2. Of those that a mesh axis runs over, the one named last changes fastest.
Arguments:
- image: bfloat16 [2048, 3072], P('seq', 'tp'), may hold values from -6 to 6
- text: bfloat16 [2, 1024, 3072], P('cfg', 'seq', 'tp'), may hold values from -6 to 6
- modulation: float32 [2, 2, 3, 3072], P('cfg'), may hold values from -3 to 3
- w_qkv: bfloat16 [3072, 4608], P('seq', 'tp'), may hold values from -0.109375 to 0.109375
- q_gain: float32 [128], replicated, may hold values from 0.5 to 12, as said below
- k_gain: float32 [128], replicated, may hold values from 0.5 to 12, as said below
- w_proj: bfloat16 [1536, 3072], P('tp', 'seq'), may hold values from -0.15625 to 0.15625
- text_len: int32 [2, 2], replicated, may hold values from 1 to 512
- text_tiles: int32 [2, 2, 4], replicated, may hold values from 0 to 3, each once within a row
- step_index: int32 [2], replicated, may hold values from 0 to 27
Outputs:
- guided: float32 [2048, 3072], P('seq', ('cfg', 'tp'))
- latent_next: float32 [2048, 3072], P('seq', ('cfg', 'tp'))
Inputs may be any that keep to these rules, and one draw needn't show every extreme that they name: `q_gain`: each query and key norm gain is positive. `k_gain`: each query and key norm gain is positive. `text_tiles`: each row of four is an order of 0 to 3.
All inputs are finite; a program needn't handle non-finite values.
Results may differ from a plain program's by a relative error of at most 0.015.
The roundings to bfloat16 on the way count: a program that leaves them out, or rounds other values in their place, can miss the bound.
Values may be sent and summed in bfloat16 or wider, within the bound.
A program may use at most 128 MiB of HBM per device.

v0:
```python
import jax
import jax.numpy as jnp
from jax import lax
from jax.sharding import PartitionSpec as P

HD = 128
STEPS = 28


GUIDANCE = 4.0
SHIFT_FACTOR = 3.0
EPSILON = 1e-06


def from_partner(block, axis, stride):
    count = lax.axis_size(axis)
    route = []
    for low in range(count):
        high = low | 1 << stride
        if high != low and high < count:
            route += [(low, high), (high, low)]
    return lax.ppermute(block, axis, route)


def layer_norm(rows):
    mean_value = jnp.mean(rows, axis=-1, keepdims=True)
    centred = rows - mean_value
    spread = jnp.mean(centred * centred, axis=-1, keepdims=True)
    return centred * lax.rsqrt(spread + EPSILON)


def head_norm(matrix, scaling):
    strength = jnp.mean(matrix * matrix, axis=-1, keepdims=True)
    return (matrix * lax.rsqrt(strength + EPSILON) * scaling).astype(jnp.bfloat16)


def sigma_of(position):
    remaining = 1.0 - position / STEPS
    return SHIFT_FACTOR * remaining / (1.0 + (SHIFT_FACTOR - 1.0) * remaining)


def local(image, text, modulation, w_qkv, q_gain, k_gain, w_proj, text_len, text_tiles, step_index):
    cfg_pos = lax.axis_index("cfg")
    seq_pos = lax.axis_index("seq")
    tp_pos = lax.axis_index("tp")
    tp_count = lax.axis_size("tp")
    prompt = seq_pos // 2
    within = seq_pos % 2
    image_full, text_full = (
        lax.all_gather(image, "tp", axis=1, tiled=True),
        lax.all_gather(text, "tp", axis=2, tiled=True),
    )
    text_rows = text_full[0]
    img_rows = image_full.shape[0]
    txt_rows = text_rows.shape[0]
    width = image_full.shape[1]
    mods = lax.dynamic_index_in_dim(modulation[0], prompt, 0, keepdims=False)
    rows_all = jnp.concatenate([image_full, text_rows], 0).astype(jnp.float32)
    normed = ((1.0 + mods[1]) * layer_norm(rows_all) + mods[0]).astype(jnp.bfloat16)
    heads_dev = w_qkv.shape[1] // (3 * HD)
    piece = lax.all_gather(w_qkv, "seq", axis=0, tiled=True)
    count = piece.shape[0]
    blocks = piece.reshape(count, heads_dev, 3, HD)
    query_weight = blocks[:, :, 0].reshape(count, heads_dev * HD)
    pair_weight = blocks[:, :, 1:].reshape(count, heads_dev * 2 * HD)
    query_sum = jnp.dot(normed[:img_rows], query_weight, preferred_element_type=jnp.float32)
    pair_sum = jnp.dot(normed, pair_weight, preferred_element_type=jnp.float32)
    query = head_norm(query_sum.reshape(img_rows, heads_dev, HD), q_gain)
    pairs = pair_sum.reshape(-1, heads_dev, 2, HD)
    keys_own = head_norm(pairs[:, :, 0], k_gain)
    values_own = pairs[:, :, 1].astype(jnp.bfloat16)
    keys_far, values_far = from_partner((keys_own, values_own), "seq", 0)
    length_now = lax.dynamic_slice(text_len, (cfg_pos, prompt), (1, 1))[0, 0]
    order_row = lax.dynamic_slice(text_tiles, (cfg_pos, prompt, 0), (1, 1, 4))[0, 0]
    tile_rows = txt_rows // 2
    offsets = jnp.arange(tile_rows, dtype=jnp.int32)

    def text_live(slot_half):
        tile_ids = lax.dynamic_slice_in_dim(order_row, 2 * slot_half, 2, 0)
        positions = (tile_ids[:, None] * tile_rows + offsets[None, :]).reshape(txt_rows)
        return positions < length_now

    image_live = jnp.ones((img_rows,), bool)
    live_keys = jnp.concatenate([image_live, text_live(within), image_live, text_live(1 - within)])
    keys_all = jnp.concatenate([keys_own, keys_far], 0)
    values_all = jnp.concatenate([values_own, values_far], 0)
    scores = jnp.einsum(
        "qhd,khd->hqk", query, keys_all, preferred_element_type=jnp.float32
    ) * HD ** (-0.5)
    scores = jnp.where(live_keys[None, None, :], scores, -jnp.inf)
    row_max = jnp.max(scores, axis=-1, keepdims=True)
    exps = jnp.exp(scores - row_max)
    probs = (exps / jnp.sum(exps, axis=-1, keepdims=True)).astype(jnp.bfloat16)
    attended = jnp.einsum("hqk,khd->qhd", probs, values_all, preferred_element_type=jnp.float32)
    attended = attended.astype(jnp.bfloat16).reshape(img_rows, heads_dev * HD)
    half_width = width // 2
    block = half_width // tp_count
    projected = jnp.dot(
        attended,
        lax.all_gather(w_proj, "seq", axis=1, tiled=True),
        preferred_element_type=jnp.float32,
    )
    summed = lax.psum(projected.astype(jnp.bfloat16), "tp").astype(jnp.float32)
    shares = lax.dynamic_slice_in_dim(
        summed.reshape(img_rows, 2, half_width), tp_pos * block, block, 2
    )
    image_block = lax.dynamic_slice_in_dim(
        image_full.reshape(img_rows, 2, half_width), tp_pos * block, block, 2
    ).astype(jnp.float32)
    gate_block = lax.dynamic_slice_in_dim(mods[2].reshape(2, half_width), tp_pos * block, block, 1)
    velocity = (image_block + gate_block[None] * shares).astype(jnp.bfloat16)
    paired = lax.all_to_all(velocity, "cfg", split_axis=1, concat_axis=1, tiled=True)
    cond_velocity = paired[:, 0].astype(jnp.float32)
    uncond_velocity = paired[:, 1].astype(jnp.float32)
    guided = uncond_velocity + GUIDANCE * (cond_velocity - uncond_velocity)
    step_now = lax.dynamic_index_in_dim(step_index, prompt, 0, keepdims=False).astype(jnp.float32)
    step_size = sigma_of(step_now + 1.0) - sigma_of(step_now)
    own_image = lax.dynamic_index_in_dim(image_block, cfg_pos, 1, keepdims=False)
    latent_next = own_image + step_size * guided
    return (guided, latent_next)


def solution(mesh):
    in_specs = (
        P("seq", "tp"),
        P("cfg", "seq", "tp"),
        P("cfg", None, None, None),
        P("seq", "tp"),
        P(),
        P(),
        P("tp", "seq"),
        P(),
        P(),
        P(),
    )
    out_specs = (P("seq", ("cfg", "tp")), P("seq", ("cfg", "tp")))
    return jax.shard_map(local, mesh=mesh, in_specs=in_specs, out_specs=out_specs, check_vma=False)
```

profile of v0, /device:TPU:0, one launch (start us, length us, event | category | flops | bytes accessed | tf_op | source)
XLA Modules:
  0.0 368.3 jit_solution(9521599123961812450)
XLA Ops:
  7.2 0.7 all-gather.7.cloned.1.call-update
  8.0 0.7 all-gather.5.cloned.1.call-update
  8.7 3.9 %copy.19 = bf16[768,1152]{0,1:T(8,128)(2,1)} copy(bf16[768,1152]{1,0:T(8,128)(2,1)} %param.13) | data formatting | bytes 3538944 | tf_op args[3]
  12.7 0.5 all-gather.11.cloned.1.call-update
  13.3 0.6 dynamic_slice.35
  14.1 0.7 compare_bitcast_fusion
  14.8 17.2 %all-gather.7.cloned.1.call-done = bf16[1,256,3072]{2,1,0:T(8,128)(2,1)} async-done(((bf16[1,256,768]{2,1,0:T(8,128)(2,1)}), bf16[1,256,3072]{2,1,0:T(8,128)(2,1)}) %all-gather.7.cloned.1.call-update) | async-done | bytes 1572880 | tf_op jit(solution)/shard_map/all_gather | solution.py:51
  32.0 30.1 %all-gather.5.cloned.1.call-done = bf16[512,3072]{1,0:T(8,128)(2,1)} async-done(((bf16[512,768]{1,0:T(8,128)(2,1)}), bf16[512,3072]{1,0:T(8,128)(2,1)}) %all-gather.5.cloned.1.call-update) | async-done | bytes 3145744 | tf_op jit(solution)/shard_map/all_gather | solution.py:50
  62.1 3.2 convert_reduce_fusion
  65.4 0.5 copy-done.1
  65.9 2.8 fusion.3
  68.7 6.6 %fusion.6 = bf16[768,3072]{1,0:T(8,128)(2,1)} fusion(f32[3072]{0:T(1024)S(1)} %bitcast.77, f32[768]{0:T(1024)S(1)} %add_rsqrt_fusion.2, f32[768]{0:T(1024)S(1)} %broadcast_multiply_fusion, f32[3072]{0:T(1024)S(1)} %bitcast.76, bf16[256,3072]{1,0:T(8,128)(2,1)S(1)} %bitcast.73, bf16[512,3072]{1,0:T(8,128)(2,1)S(1)} %copy-done), kind=kLoop, calls=%fused_computation.8 | loop fusion | flops 21233664 | bytes 9467904 | tf_op jit(solution)/shard_map/convert_element_type | solution.py:59
  75.3 116.6 %all-gather.9.cloned.1.call-done = bf16[3072,1152]{0,1:T(8,128)(2,1)} async-done(((bf16[768,1152]{0,1:T(8,128)(2,1)}), bf16[3072,1152]{0,1:T(8,128)(2,1)}) %all-gather.9.cloned.1.call-update) | async-done | bytes 7077904 | tf_op jit(solution)/shard_map/all_gather | solution.py:61
  191.9 6.6 %fusion.8 = f32[768,3,2,128]{3,0,2,1:T(8,128)S(1)} fusion(bf16[3072,3,3,128]{0,3,2,1:T(8,128)(2,1)} %bitcast.78, bf16[768,3072]{1,0:T(8,128)(2,1)} %fusion.6), kind=kOutput, calls=%fused_computation.14 | convolution fusion | flops 3623878656 | bytes 11796480 | tf_op jit(solution)/shard_map/dot_general | solution.py:67
  198.6 0.4 multiply_reduce_fusion
  199.5 2.1 collective-permute-start
  201.6 3.1 multiply_reduce_fusion.1
  204.7 37.2 %collective-permute-done.1 = bf16[768,3,128]{2,0,1:T(8,128)(2,1)S(1)} collective-permute-done((bf16[768,3,128]{2,0,1:T(8,128)(2,1)S(1)}, bf16[768,3,128]{2,0,1:T(8,128)(2,1)S(1)}, u32[]{:S(2)}, u32[]{:S(2)}) %collective-permute-start.1) | collective-permute-done | bytes 589856 | tf_op jit(solution)/shard_map/ppermute | solution.py:22
  242.0 1.5 fusion.19
  243.5 5.2 %fusion.31 = (f32[3,512]{1,0:T(4,128)S(1)}, f32[3,512,1536]{2,1,0:T(8,128)}) fusion(f32[3,512,1536]{2,1,0:T(8,128)S(1)} %fusion.19, pred[1536]{0:T(1024)(128)(4,1)S(1)} %pad_add_fusion), kind=kOutput, calls=%fused_computation.69 | output fusion | flops 14157311 | bytes 18882048 | tf_op jit(solution)/shard_map/sub | solution.py:92
  248.7 16.6 %collective-permute-done = bf16[768,3,128]{2,0,1:T(8,128)(2,1)S(1)} collective-permute-done((bf16[768,3,128]{2,0,1:T(8,128)(2,1)S(1)}, bf16[768,3,128]{2,0,1:T(8,128)(2,1)S(1)}, u32[]{:S(2)}, u32[]{:S(2)}) %collective-permute-start) | collective-permute-done | bytes 589856 | tf_op jit(solution)/shard_map/ppermute | solution.py:22
  265.3 6.2 %fusion.15 = bf16[3,128,512]{2,1,0:T(8,128)(2,1)} fusion(f32[3,512,1536]{2,1,0:T(8,128)} %get-tuple-element.12, f32[3,512]{1,0:T(4,128)S(1)} %get-tuple-element.11, bf16[768,3,128]{2,0,1:T(8,128)(2,1)S(1)} %collective-permute-done, bf16[768,3,128]{2,0,1:T(8,128)(2,1)S(1)} %fusion.24), kind=kOutput, calls=%fused_computation.27 | convolution fusion | flops 611254272 | bytes 11016192 | tf_op jit(solution)/shard_map/hqk,khd->qhd/dot_general | solution.py:94
  271.5 3.6 convolution_convert_fusion
  275.1 1.9 copy.32
  277.1 3.6 reshape.129
  280.8 1.7 constant_dynamic-slice_fusion.2
  282.5 61.3 %all-reduce.2.cloned.1.call-done = bf16[512,2,1536]{2,0,1:T(8,128)(2,1)} async-done(((bf16[512,2,1536]{2,0,1:T(8,128)(2,1)}), bf16[512,2,1536]{2,0,1:T(8,128)(2,1)}) %all-reduce.2.cloned.1.call-update) | async-done | bytes 3145744 | tf_op jit(solution)/shard_map/psum | solution.py:103
  343.8 2.2 add_convert_fusion
  346.0 3.5 all-to-all-start
  349.6 0.6 dynamic_slice.39
  351.0 9.5 %all-to-all-done = bf16[512,2,384]{2,0,1:T(8,128)(2,1)S(1)} async-done(((bf16[512,2,384]{2,0,1:T(8,128)(2,1)}), bf16[512,2,384]{2,0,1:T(8,128)(2,1)S(1)}, u32[]{:S(2)}, u32[]{:S(2)}) %all-to-all-start) | async-done | bytes 786464 | tf_op jit(solution)/shard_map/all_to_all | solution.py:112
  360.5 1.3 bitcast_add_fusion
  (39 shorter events, 1.2 us)
Async XLA Ops:
  7.2 6.2 %copy-start.7 = (s32[2,2]{1,0:T(2,128)S(1)}, s32[2,2]{1,0:T(2,128)}, u32[]{:S(2)}) copy-start(s32[2,2]{1,0:T(2,128)} %param.17) | copy-start | bytes 52
  7.2 6.7 %copy-start.3 = (f32[1,2,3,3072]{3,1,2,0:T(2,128)S(1)}, f32[1,2,3,3072]{3,1,2,0:T(2,128)}, u32[]{:S(2)}) copy-start(f32[1,2,3,3072]{3,1,2,0:T(2,128)} %param.12) | copy-start | bytes 221188
  7.2 6.8 %copy-start.5 = (s32[2,2,4]{2,1,0:T(2,128)S(1)}, s32[2,2,4]{2,1,0:T(2,128)}, u32[]{:S(2)}) copy-start(s32[2,2,4]{2,1,0:T(2,128)} %param.18) | copy-start | bytes 196
  7.2 24.8 %all-gather.7.cloned.1.call-start = ((), (), s32[]{:S(2)}) async-start(), calls=%async_computation.2 | async-start | bytes 1966080 | tf_op jit(solution)/shard_map/all_gather | solution.py:51
  7.9 54.2 %all-gather.5.cloned.1.call-start = ((), (), s32[]{:S(2)}) async-start(), calls=%async_computation.1 | async-start | bytes 3932160 | tf_op jit(solution)/shard_map/all_gather | solution.py:50
  8.7 183.3 %all-gather.9.cloned.1.call-start = ((), (), s32[]{:S(2)}) async-start(), calls=%async_computation.3 | async-start | bytes 8847360 | tf_op jit(solution)/shard_map/all_gather | solution.py:61
  12.6 258.9 %all-gather.11.cloned.1.call-start = ((), (), s32[]{:S(2)}) async-start(), calls=%async_computation.4 | async-start | bytes 2949120 | tf_op jit(solution)/shard_map/all_gather | solution.py:100
  13.2 330.6 %all-reduce.2.cloned.1.call-start = ((), (), s32[]{:S(2)}) async-start(), calls=%async_computation.5 | async-start | bytes 6291456 | tf_op jit(solution)/shard_map/psum | solution.py:103
  62.1 3.3 copy-start
  62.1 3.8 %copy-start.1 = (bf16[1,256,3072]{2,1,0:T(8,128)(2,1)S(1)}, bf16[1,256,3072]{2,1,0:T(8,128)(2,1)}, u32[]{:S(2)}) copy-start(bf16[1,256,3072]{2,1,0:T(8,128)(2,1)} %all-gather.7.cloned.1.call-done) | copy-start | bytes 4718596
  191.9 7.0 %copy-start.6 = (f32[128]{0:T(128)S(1)}, f32[128]{0:T(128)}, u32[]{:S(2)}) copy-start(f32[128]{0:T(128)} %param.15) | copy-start | bytes 1540
  191.9 9.7 %copy-start.2 = (bf16[768,3072]{1,0:T(8,128)(2,1)S(1)}, bf16[768,3072]{1,0:T(8,128)(2,1)}, u32[]{:S(2)}) copy-start(bf16[768,3072]{1,0:T(8,128)(2,1)} %fusion.6) | copy-start | bytes 14155780
  199.4 42.6 %collective-permute-start.1 = (bf16[768,3,128]{2,0,1:T(8,128)(2,1)S(1)}, bf16[768,3,128]{2,0,1:T(8,128)(2,1)S(1)}, u32[]{:S(2)}, u32[]{:S(2)}) collective-permute-start(bf16[768,3,128]{2,0,1:T(8,128)(2,1)S(1)} %multiply_convert_fusion), channel_id=1, source_target_pairs={{0,4},{4,0},{8,12},{12,8},{1,5},{5,1},{9,13},{13,9},{2,6},{6,2},{1... | collective-permute-start | bytes 1769480 | tf_op jit(solution)/shard_map/ppermute | solution.py:22
  199.5 42.4 %copy-start.4 = (f32[128]{0:T(128)S(1)}, f32[128]{0:T(128)}, u32[]{:S(2)}) copy-start(f32[128]{0:T(128)} %param.14) | copy-start | bytes 1540
  199.5 65.7 %collective-permute-start = (bf16[768,3,128]{2,0,1:T(8,128)(2,1)S(1)}, bf16[768,3,128]{2,0,1:T(8,128)(2,1)S(1)}, u32[]{:S(2)}, u32[]{:S(2)}) collective-permute-start(bf16[768,3,128]{2,0,1:T(8,128)(2,1)S(1)} %fusion.24), channel_id=1, source_target_pairs={{0,4},{4,0},{8,12},{12,8},{1,5},{5,1},{9,13},{13,9},{2,6},{6,2},{1... | collective-permute-start | bytes 1769480 | tf_op jit(solution)/shard_map/ppermute | solution.py:22
  277.1 72.4 %copy-start.8 = (s32[2]{0:T(128)S(1)}, s32[2]{0:T(128)}, u32[]{:S(2)}) copy-start(s32[2]{0:T(128)} %param.19) | copy-start | bytes 28
  346.0 14.5 %all-to-all-start = ((bf16[512,2,384]{2,0,1:T(8,128)(2,1)}), bf16[512,2,384]{2,0,1:T(8,128)(2,1)S(1)}, u32[]{:S(2)}, u32[]{:S(2)}) async-start(bf16[512,2,384]{2,0,1:T(8,128)(2,1)} %add_convert_fusion), calls=%async_computation | async-start | bytes 1572864 | tf_op jit(solution)/shard_map/all_to_all | solution.py:112
Sparse Core Ops, SparseCore 0:
  9.6 22.3 all-gather.6
  33.5 28.5 all-gather.4
  63.7 128.1 all-gather.8
  193.4 69.8 all-gather.10
  277.2 66.5 all-reduce.1
where the time goes:
time: 369 us; the launch traced here: 368 us
  waiting for transfers between devices  290 us (79%)
  other arithmetic  23.1 us (6%)
  matrix products  21.1 us (6%)
  between operations  14.8 us (4%)
  local copies, waits for them, and re-layouts  13.1 us (4%)
  starting transfers between devices  5.87 us (2%)
    all_gather x1, waiting for transfers between devices, local(): piece = lax.all_gather(w_qkv, 'seq', axis=0, tiled=True)  117 us
    psum x1, waiting for transfers between devices, local(): summed = lax.psum(projected.astype(jnp.bfloat16), 'tp').astype(jnp.float32)  61.3 us
    ppermute x2, waiting for transfers between devices, from_partner(): return lax.ppermute(block, axis, route)  53.8 us
    all_gather x1, waiting for transfers between devices, local(): lax.all_gather(image, 'tp', axis=1, tiled=True)  30.1 us
    all_gather x1, waiting for transfers between devices, local(): lax.all_gather(text, 'tp', axis=2, tiled=True)  17.2 us
    all_to_all x1, waiting for transfers between devices, local(): lax.all_to_all(velocity, 'cfg', split_axis=1, concat_axis=1, tiled=True)  9.48 us
  transfers between devices with their start and end apart: 8, of which 7 were waited for; matrix products, arithmetic and copies ran while one was open for 13% of the time, Pallas kernels for 0%

commit v1 on v0

v1 whole, which is shorter than its diff:
```python
import functools

import jax
import jax.numpy as jnp
from jax import lax
from jax.experimental import pallas as pl
from jax.experimental.pallas import tpu as pltpu
from jax.sharding import PartitionSpec as P

HD = 128
STEPS = 28


GUIDANCE = 4.0
SHIFT_FACTOR = 3.0
EPSILON = 1e-06


def from_partner(block, axis, stride):
    count = lax.axis_size(axis)
    route = []
    for low in range(count):
        high = low | 1 << stride
        if high != low and high < count:
            route += [(low, high), (high, low)]
    return lax.ppermute(block, axis, route)


def layer_norm(rows):
    mean_value = jnp.mean(rows, axis=-1, keepdims=True)
    centred = rows - mean_value
    spread = jnp.mean(centred * centred, axis=-1, keepdims=True)
    return centred * lax.rsqrt(spread + EPSILON)


def head_norm(matrix, scaling):
    strength = jnp.mean(matrix * matrix, axis=-1, keepdims=True)
    return (matrix * lax.rsqrt(strength + EPSILON) * scaling).astype(jnp.bfloat16)


def sigma_of(position):
    remaining = 1.0 - position / STEPS
    return SHIFT_FACTOR * remaining / (1.0 + (SHIFT_FACTOR - 1.0) * remaining)


MESH = pl.DeviceIdType.MESH


class Sender:
    def __init__(self):
        self.pending = []

    def push(self, src, dst, send, recv, to, when=None):
        copy = pltpu.make_async_remote_copy(
            src_ref=src, dst_ref=dst, send_sem=send, recv_sem=recv, device_id=to, device_id_type=MESH
        )
        guarded(when, copy.start)
        self.pending.append((when, copy.wait_send))

    def local(self, src, dst, sem, when=None):
        copy = pltpu.make_async_copy(src, dst, sem)
        guarded(when, copy.start)
        self.pending.append((when, copy.wait))

    def finish(self):
        for when, wait in self.pending:
            guarded(when, wait)


def guarded(when, act):
    if when is None:
        act()
    else:
        pl.when(when)(act)


def arrive(dst, sem, when=None):
    copy = pltpu.make_async_copy(dst, dst, sem)
    guarded(when, copy.wait)


def greet(partners):
    barrier = pltpu.get_barrier_semaphore()
    for device in partners:
        pl.semaphore_signal(barrier, inc=1, device_id=device, device_id_type=MESH)
    pl.semaphore_wait(barrier, len(partners))


def gather_kernel(
    n, tps, image, text, wqkv, wproj, acts, wfull, wcols, iblock,
    act_send, act_recv, fwd_send, z_send, z_recv, x_send, x_recv, k_send, k_recv, kx_send, kx_recv,
    own_send, own_recv, p_send, p_recv, i_send, i_recv,
):
    c, s, t = lax.axis_index("cfg"), lax.axis_index("seq"), lax.axis_index("tp")
    w, k, y = s % 2, t % 2, t // 2
    img, feats = image.shape
    txt = text.shape[1]
    depth, _ = wqkv.shape
    half = depth // 2
    chunk = half // 2 if (half // 2) % 16 == 0 else half
    chunks = half // chunk
    other_s = s + 1 - 2 * w
    other_k = t + 1 - 2 * k
    greet(
        [(c, (s + ds) % n, (t + dt) % tps) for ds in range(n) for dt in range(tps) if (ds, dt) != (0, 0)]
        + [(1 - c, s, t)]
    )
    out = Sender()
    is_main = k == w

    def rows_of(block, part, j):
        return pl.ds(pl.multiple_of(block * depth + part * half + j * chunk, 16), chunk)

    for d in range(1, n):
        to = (s + d) % n
        for j in range(chunks):
            out.push(
                wqkv.at[pl.ds(pl.multiple_of(c * half + j * chunk, 16), chunk)],
                wfull.at[rows_of(s, c, j)],
                z_send.at[d, j], z_recv.at[d, j], (c, to, t), when=(to % 2) == k,
            )
    def act_parts(block):
        cols = pl.ds(pl.multiple_of(block * feats, 128), feats)
        return [(0, acts.at[pl.ds(0, img), cols]), (1, acts.at[pl.ds(img, txt), cols])]

    sources = [image, text.at[0]]
    for part, dst in act_parts(t):
        out.push(sources[part], dst, act_send.at[tps // 2, part], act_recv.at[t, part], (c, other_s, 2 * y + w))
        for dy in range(1, tps // 2):
            to_y = (y + dy) % (tps // 2)
            out.push(sources[part], dst, act_send.at[dy, part], act_recv.at[t, part], (c, s, 2 * to_y + w))
        out.push(sources[part], dst, act_send.at[0, part], act_recv.at[t, part], (c, s, other_k), when=k != w)
        out.local(sources[part], dst, act_recv.at[t, part], when=k == w)
    own_rows = wfull.at[pl.ds(pl.multiple_of(s * depth, 16), depth)]
    out.local(wqkv, own_rows, own_recv, when=is_main)
    out.push(wqkv, own_rows, own_send, own_recv, (c, s, other_k), when=is_main)
    rows, width = wproj.shape
    pieces, _, piece = wcols.shape
    per = width // piece
    total_half = (n * width) // 2
    mine = (s * width) // total_half == c
    first = (s * width - c * total_half) // piece
    for h in range(per):
        index = jnp.maximum(first + h, 0)
        to_t = (index // pieces) % tps
        slot = index % pieces
        for ds in range(n):
            to_s = (s + ds) % n
            dst = wcols.at[slot, pl.ds(pl.multiple_of(t * rows, 16), rows)]
            src = wproj.at[:, pl.ds(h * piece, piece)] if per > 1 else wproj
            if ds == 0:
                same = to_t == t
                out.push(src, dst, p_send.at[ds, h], p_recv.at[slot, t], (c, to_s, to_t), when=mine & (to_t != t))
                out.local(src, dst, p_recv.at[slot, t], when=mine & same)
            else:
                out.push(src, dst, p_send.at[ds, h], p_recv.at[slot, t], (c, to_s, to_t), when=mine)
    block = iblock.shape[1]
    for h in range(2):
        index = 2 * t + h
        to_c, to_t = index // tps, index % tps
        src = image.at[:, pl.ds(h * block, block)]
        out.push(src, iblock, i_send.at[h], i_recv, (c, s, to_t), when=(to_c == c) & (to_t != t))
        out.local(src, iblock, i_recv, when=(to_c == c) & (to_t == t))

    far = k != w
    for dk in range(2):
        block_t = 2 * y + dk
        for part, dst in act_parts(block_t):
            arrive(dst, act_recv.at[block_t, part], when=far)
            for dy in range(1, tps // 2):
                to_y = (y + dy) % (tps // 2)
                out.push(
                    dst, dst, fwd_send.at[dk, dy, part], act_recv.at[block_t, part], (c, s, 2 * to_y + k), when=far
                )
    for d in range(1, n):
        origin = (s - d + n) % n
        for j in range(chunks):
            dst = wfull.at[rows_of(origin, c, j)]
            arrive(dst, z_recv.at[d, j], when=is_main)
            out.push(dst, dst, x_send.at[d, j], x_recv.at[d, j], (1 - c, s, t), when=is_main)
            out.push(dst, dst, k_send.at[d, j], k_recv.at[d, j], (c, s, other_k), when=is_main)
    for d in range(1, n):
        origin = (s - d + n) % n
        for j in range(chunks):
            dst = wfull.at[rows_of(origin, 1 - c, j)]
            arrive(dst, x_recv.at[d, j], when=is_main)
            out.push(dst, dst, kx_send.at[d, j], kx_recv.at[d, j], (c, s, other_k), when=is_main)
    for d in range(1, n):
        origin = (s - d + n) % n
        for j in range(chunks):
            arrive(wfull.at[rows_of(origin, c, j)], k_recv.at[d, j], when=~is_main)
            arrive(wfull.at[rows_of(origin, 1 - c, j)], kx_recv.at[d, j], when=~is_main)
    arrive(own_rows, own_recv, when=~is_main)
    for block_t in range(tps):
        for part, dst in act_parts(block_t):
            waited = far & (block_t // 2 == y)
            own = (k == w) & (block_t == t)
            arrive(dst, act_recv.at[block_t, part], when=~(waited | own))
    needed_first = t * pieces
    for slot in range(pieces):
        own_source = ((c * total_half + t * pieces * piece + slot * piece) // width) == s
        for from_t in range(tps):
            dst = wcols.at[slot, pl.ds(from_t * rows, rows)]
            arrive(dst, p_recv.at[slot, from_t], when=~(own_source & (from_t == t)))
    own_image = (c * tps + t) // 2 == t
    arrive(iblock, i_recv, when=~own_image)
    out.finish()


def gather_all(n, tps, image, text, wqkv, wproj):
    img, feats = image.shape
    txt = text.shape[1]
    depth, cols = wqkv.shape
    rows, width = wproj.shape
    block = feats // 2
    piece = min(width, block)
    pieces = block // piece
    half = depth // 2
    chunks = 2 if (half // 2) % 16 == 0 else 1
    per = width // piece
    dma = pltpu.SemaphoreType.DMA
    any_space = pl.BlockSpec(memory_space=pl.ANY)
    bf16 = jnp.bfloat16
    return pl.pallas_call(
        functools.partial(gather_kernel, n, tps),
        out_shape=(
            jax.ShapeDtypeStruct((img + txt, tps * feats), bf16),
            jax.ShapeDtypeStruct((n * depth, cols), bf16),
            jax.ShapeDtypeStruct((pieces, tps * rows, piece), bf16),
            jax.ShapeDtypeStruct((img, block), bf16),
        ),
        in_specs=[any_space] * 4,
        out_specs=(any_space,) * 4,
        scratch_shapes=[
            dma((tps // 2 + 1, 2)), dma((tps, 2)), dma((2, tps // 2, 2)),
            dma((n, chunks)), dma((n, chunks)), dma((n, chunks)), dma((n, chunks)),
            dma((n, chunks)), dma((n, chunks)), dma((n, chunks)), dma((n, chunks)),
            dma, dma, dma((n, per)), dma((pieces, tps)), dma((2,)), dma,
        ],
        compiler_params=pltpu.CompilerParams(collective_id=0, has_side_effects=True),
    )(image, text, wqkv, wproj)


def exchange_kernel(n, tps, attended, gathered, send, recv, fwd_send, fwd_recv):
    c, s, t = lax.axis_index("cfg"), lax.axis_index("seq"), lax.axis_index("tp")
    w, k, y = s % 2, t % 2, t // 2
    ys = tps // 2
    plane = s - w + k
    cols = attended.shape[1]
    other_k = t + 1 - 2 * k
    greet(
        [
            ((c + dc) % 2, s - w + (w + ds) % 2, (t + dt) % tps)
            for dc in range(2) for ds in range(2) for dt in range(tps) if (dc, ds, dt) != (0, 0, 0)
        ]
    )
    out = Sender()

    def place(half, head):
        return gathered.at[half, :, pl.ds(pl.multiple_of(head * cols, 128), cols)]

    for dc in (1, 0):
        for dy in reversed(range(ys)):
            to = ((c + dc) % 2, plane, 2 * ((y + dy) % ys) + w)
            dst = place(c, 2 * y + w)
            if dc == 0 and dy == 0:
                out.push(attended, dst, send.at[dc, dy], recv.at[dc, dy], to, when=k != w)
                out.local(attended, dst, recv.at[dc, dy], when=k == w)
            else:
                out.push(attended, dst, send.at[dc, dy], recv.at[dc, dy], to)
    for dc in range(2):
        for dy in range(ys):
            half, from_y = (c - dc + 2) % 2, (y - dy + ys) % ys
            dst = place(half, 2 * from_y + k)
            if dc == 0 and dy == 0:
                arrive(dst, recv.at[dc, dy], when=k != w)
                out.push(dst, dst, fwd_send.at[dc, dy], fwd_recv.at[dc, dy], (c, s, other_k), when=k != w)
                out.push(attended, dst, fwd_send.at[dc, dy], fwd_recv.at[dc, dy], (c, s, other_k), when=k == w)
            else:
                arrive(dst, recv.at[dc, dy])
                out.push(dst, dst, fwd_send.at[dc, dy], fwd_recv.at[dc, dy], (c, s, other_k))
    for dc in range(2):
        for dy in range(ys):
            half, from_y = (c - dc + 2) % 2, (y - dy + ys) % ys
            arrive(place(half, 2 * from_y + 1 - k), fwd_recv.at[dc, dy])
    out.finish()


def exchange(n, tps, attended):
    dma = pltpu.SemaphoreType.DMA
    any_space = pl.BlockSpec(memory_space=pl.ANY)
    rows, cols = attended.shape
    return pl.pallas_call(
        functools.partial(exchange_kernel, n, tps),
        out_shape=jax.ShapeDtypeStruct((2, rows, tps * cols), jnp.bfloat16),
        in_specs=[any_space],
        out_specs=any_space,
        scratch_shapes=[dma((2, tps // 2))] * 4,
        compiler_params=pltpu.CompilerParams(collective_id=1, has_side_effects=True),
    )(attended)


def local(image, text, modulation, w_qkv, q_gain, k_gain, w_proj, text_len, text_tiles, step_index):
    cfg_pos = lax.axis_index("cfg")
    seq_pos = lax.axis_index("seq")
    tp_pos = lax.axis_index("tp")
    tp_count = lax.axis_size("tp")
    seq_count = lax.axis_size("seq")
    prompt = seq_pos // 2
    part = tp_pos % 2
    mods = lax.dynamic_index_in_dim(modulation[0], prompt, 0, keepdims=False)
    block = image.shape[1] // 2
    width = image.shape[1] * tp_count
    gate_rows = mods[2].reshape(2 * tp_count, block)
    gate_own = lax.dynamic_index_in_dim(gate_rows, cfg_pos * tp_count + tp_pos, 0, keepdims=False)
    gate_sent = lax.dynamic_index_in_dim(gate_rows, (1 - cfg_pos) * tp_count + tp_pos, 0, keepdims=False)
    gate_far = from_partner(gate_sent, "cfg", 0)
    acts, piece, wcols, image_block = gather_all(seq_count, tp_count, image, text, w_qkv, w_proj)
    img_rows = image.shape[0]
    txt_rows = text.shape[1]
    normed = ((1.0 + mods[1]) * layer_norm(acts.astype(jnp.float32)) + mods[0]).astype(jnp.bfloat16)
    heads_dev = w_qkv.shape[1] // (3 * HD)
    count = piece.shape[0]
    blocks = piece.reshape(count, heads_dev, 3, HD)
    query_weight = blocks[:, :, 0].reshape(count, heads_dev * HD)
    pair_weight = blocks[:, :, 1:].reshape(count, heads_dev * 2 * HD)
    query_sum = jnp.dot(normed[:img_rows], query_weight, preferred_element_type=jnp.float32)
    pair_sum = jnp.dot(normed, pair_weight, preferred_element_type=jnp.float32)
    query = head_norm(query_sum.reshape(img_rows, heads_dev, HD), q_gain)
    pairs = pair_sum.reshape(-1, heads_dev, 2, HD)
    keys_own = head_norm(pairs[:, :, 0], k_gain)
    values_own = pairs[:, :, 1].astype(jnp.bfloat16)
    keys_far, values_far = from_partner((keys_own, values_own), "tp", 0)
    length_now = lax.dynamic_slice(text_len, (cfg_pos, prompt), (1, 1))[0, 0]
    order_row = lax.dynamic_slice(text_tiles, (cfg_pos, prompt, 0), (1, 1, 4))[0, 0]
    tile_rows = txt_rows // 2
    offsets = jnp.arange(tile_rows, dtype=jnp.int32)

    def text_live(slot_half):
        tile_ids = lax.dynamic_slice_in_dim(order_row, 2 * slot_half, 2, 0)
        positions = (tile_ids[:, None] * tile_rows + offsets[None, :]).reshape(txt_rows)
        return positions < length_now

    image_live = jnp.ones((img_rows,), bool)
    live_keys = jnp.concatenate([image_live, text_live(part), image_live, text_live(1 - part)])
    keys_all = jnp.concatenate([keys_own, keys_far], 0)
    values_all = jnp.concatenate([values_own, values_far], 0)
    scores = jnp.einsum(
        "qhd,khd->hqk", query, keys_all, preferred_element_type=jnp.float32
    ) * HD ** (-0.5)
    scores = jnp.where(live_keys[None, None, :], scores, -jnp.inf)
    row_max = jnp.max(scores, axis=-1, keepdims=True)
    exps = jnp.exp(scores - row_max)
    probs = (exps / jnp.sum(exps, axis=-1, keepdims=True)).astype(jnp.bfloat16)
    attended = jnp.einsum("hqk,khd->qhd", probs, values_all, preferred_element_type=jnp.float32)
    attended = attended.astype(jnp.bfloat16).reshape(img_rows, heads_dev * HD)
    gathered = exchange(seq_count, tp_count, attended)
    weight = wcols[0] if wcols.shape[0] == 1 else jnp.concatenate(list(wcols), axis=1)
    projected = jnp.dot(
        gathered.reshape(2 * img_rows, -1), weight, preferred_element_type=jnp.float32
    ).reshape(2, img_rows, block)
    own_image = image_block.astype(jnp.float32)
    gates = jnp.where(cfg_pos == 0, jnp.stack([gate_own, gate_far]), jnp.stack([gate_far, gate_own]))
    velocity = (own_image[None] + gates[:, None, :] * projected).astype(jnp.bfloat16)
    cond_velocity = velocity[0].astype(jnp.float32)
    uncond_velocity = velocity[1].astype(jnp.float32)
    guided = uncond_velocity + GUIDANCE * (cond_velocity - uncond_velocity)
    step_now = lax.dynamic_index_in_dim(step_index, prompt, 0, keepdims=False).astype(jnp.float32)
    step_size = sigma_of(step_now + 1.0) - sigma_of(step_now)
    latent_next = own_image + step_size * guided
    return (guided, latent_next)


def solution(mesh):
    in_specs = (
        P("seq", "tp"),
        P("cfg", "seq", "tp"),
        P("cfg", None, None, None),
        P("seq", "tp"),
        P(),
        P(),
        P("tp", "seq"),
        P(),
        P(),
        P(),
    )
    out_specs = (P("seq", ("cfg", "tp")), P("seq", ("cfg", "tp")))
    return jax.shard_map(local, mesh=mesh, in_specs=in_specs, out_specs=out_specs, check_vma=False)
```

time: 369 us -> 199 us (0.54)
  waiting for transfers between devices: 290 us -> 0.01 us
  Pallas kernels: 0 us -> 143 us
  between operations: 14.8 us -> 1.72 us
  other arithmetic: 23.1 us -> 16.4 us
    all_gather x4 -> x0, waiting for transfers between devices: 164 us -> none  [the longest x1 117 us: local(): piece = lax.all_gather(w_qkv, 'seq', axis=0, tiled=True)]
    pallas_call x0 -> x2, Pallas kernels: none -> 143 us  [the longest x1 117 us: gather_all(): pl.pallas_call(functools.partial(gather_kernel, n, tps), out_shape=(jax.S...]
    psum x1 -> x0, waiting for transfers between devices: 61.3 us -> none  [local(): summed = lax.psum(projected.astype(jnp.bfloat16), 'tp').astype(jnp.float32)]
    ppermute x2 -> x3, waiting for transfers between devices: 53.8 us -> 0.01 us  [from_partner(): return lax.ppermute(block, axis, route)]
    pallas_call x0 -> x1, local copies, waits for them, and re-layouts: none -> 10.3 us  [gather_all(): pl.pallas_call(functools.partial(gather_kernel, n, tps), out_shape=(jax.S...]
    all_to_all x1 -> x0, waiting for transfers between devices: 9.48 us -> none  [local(): lax.all_to_all(velocity, 'cfg', split_axis=1, concat_axis=1, tiled=True)]
    convert_element_type x3 -> x2, other arithmetic: 8.89 us -> 2.69 us  [the longest x1 2.63 us: local(): ((1.0 + mods[1]) * layer_norm(acts.astype(jnp.float32)) + mods[0]).astype...]
    reshape x2 -> x1, local copies, waits for them, and re-layouts: 5.56 us -> 0.92 us  [local(): attended = attended.astype(jnp.bfloat16).reshape(img_rows, heads_dev * HD)]
  transfers between devices with their start and end apart: 8 -> 3, of which waited for: 7 -> 0; matrix products, arithmetic and copies ran while one was open for 13% -> 18% of each run, Pallas kernels for 0% -> 59%
where the time goes in v1:
time: 199 us; the launch traced here: 198 us
  Pallas kernels  143 us (72%)
  matrix products  20.2 us (10%)
  other arithmetic  16.4 us (8%)
  local copies, waits for them, and re-layouts  13.1 us (7%)
  starting transfers between devices  3.64 us (2%)
    pallas_call x1, Pallas kernels, gather_all(): pl.pallas_call(functools.partial(gather_kernel, n, tps), out_shape=(jax.S...  117 us
    pallas_call x1, Pallas kernels, exchange(): pl.pallas_call(functools.partial(exchange_kernel, n, tps), out_shape=jax....  26.5 us
    pallas_call x1, local copies, waits for them, and re-layouts, gather_all(): pl.pallas_call(functools.partial(gather_kernel, n, tps), out_shape=(jax.S...  10.3 us
    dot_general x1, matrix products, local(): jnp.einsum('hqk,khd->qhd', probs, values_all, preferred_element_type=jnp....  5.68 us
    sub x1, other arithmetic, local(): exps = jnp.exp(scores - row_max)  5.42 us
    dot_general x1, matrix products, local(): jnp.dot(normed[:img_rows], query_weight, preferred_element_type=jnp.float32)  4.09 us
    dot_general x1, matrix products, local(): jnp.dot(gathered.reshape(2 * img_rows, -1), weight, preferred_element_typ...  4 us
  transfers between devices with their start and end apart: 3, of which 0 were waited for; matrix products, arithmetic and copies ran while one was open for 18% of the time, Pallas kernels for 59%

profile of v1, /device:TPU:0, one launch (start us, length us, event | category | flops | bytes accessed | tf_op | source)
XLA Modules:
  0.0 198.4 jit_solution(7536569865513301114)
XLA Ops:
  0.7 0.8 dynamic-slice_reduce_fusion
  1.5 3.0 %collective-permute-start = (f32[384]{0:T(512)S(1)}, f32[384]{0:T(512)S(1)}, u32[]{:S(2)}, u32[]{:S(2)}) collective-permute-start(f32[384]{0:T(512)S(1)} %get-tuple-element.16), channel_id=1, source_target_pairs={{0,16},{16,0},{1,17},{17,1},{2,18},{18,2},{3,19},{19,3},{4,20},{20... | collective-permute-start | bytes 4616 | tf_op jit(solution)/shard_map/ppermute | solution.py:26
  4.5 116.8 %shard_map.113 = (bf16[768,3072]{1,0:T(8,128)(2,1)}, bf16[3072,1152]{1,0:T(8,128)(2,1)}, bf16[1,1536,384]{2,1,0:T(8,128)(2,1)}, bf16[512,384]{1,0:T(8,128)(2,1)}) custom-call(bf16[512,768]{1,0:T(8,128)(2,1)} %image.1, bf16[1,256,768]{2,1,0:T(8,128)(2,1)} %text.1, bf16[768,1152]{1,0:T(8,128)(2,1)} %wqkv.1, bf16[384,768]{1,0:T(8,128)(2,1)} %wproj.1), custom_call_target="tpu_custom_call" | custom-call | tf_op jit(solution)/shard_map/pallas_call | solution.py:224
  121.3 10.3 %copy.17 = bf16[3072,1152]{0,1:T(8,128)(2,1)} copy(bf16[3072,1152]{1,0:T(8,128)(2,1)} %get-tuple-element.8) | data formatting | bytes 14155776 | tf_op jit(solution)/shard_map/pallas_call | solution.py:224
  131.6 3.2 %convert_reduce_fusion = f32[768]{0:T(1024)S(1)} fusion(bf16[768,3072]{1,0:T(8,128)(2,1)} %get-tuple-element.7), kind=kLoop, calls=%fused_computation.2 | loop fusion | flops 4717824 | bytes 4721664 | tf_op jit(solution)/shard_map/reduce_sum | solution.py:30
  134.8 0.6 copy-done
  135.4 1.4 fusion.3
  136.7 0.0 slice-start.1
  136.8 2.6 %fusion.6 = bf16[768,3072]{1,0:T(8,128)(2,1)S(1)} fusion(bf16[768,3072]{1,0:T(8,128)(2,1)S(1)} %copy-done, f32[3072]{0:T(1024)S(1)} %bitcast.75, f32[768]{0:T(1024)S(1)} %add_rsqrt_fusion.2, f32[768]{0:T(1024)S(1)} %broadcast_multiply_fusion, f32[3072]{0:T(1024)S(1)} %bitcast.74), kind=kLoop, calls=%fused_computation.8 | loop fusion | flops 14155776 | bytes 9467904 | tf_op jit(solution)/shard_map/convert_element_type | solution.py:321
  139.4 0.0 copy-start.5
  139.5 3.8 %fusion.8 = f32[768,3,2,128]{3,0,2,1:T(8,128)S(1)} fusion(bf16[3072,3,3,128]{0,3,2,1:T(8,128)(2,1)S(1)} %bitcast.72, bf16[768,3072]{1,0:T(8,128)(2,1)S(1)} %fusion.6), kind=kOutput, calls=%fused_computation.14 | convolution fusion | flops 3623878656 | bytes 11796480 | tf_op jit(solution)/shard_map/dot_general | solution.py:328
  143.3 0.1 fusion.26
  143.4 0.1 collective-permute-start.1
  143.5 0.4 multiply_reduce_fusion
  143.9 0.4 multiply_convert_fusion
  144.3 0.6 collective-permute-start.2
  144.8 0.0 copy-start.3
  144.9 4.1 %multiply_reduce_fusion.1 = (f32[512,3]{0,1:T(4,128)S(1)}, f32[512,3,128]{0,2,1:T(8,128)S(1)}) fusion(bf16[3072,3,3,128]{0,3,2,1:T(8,128)(2,1)} %bitcast.69, bf16[768,3072]{1,0:T(8,128)(2,1)} %copy-done.1), kind=kOutput, calls=%fused_computation.43 | convolution fusion | flops 1208351232 | bytes 6297600 | tf_op jit(solution)/shard_map/dot_general | solution.py:327
  149.0 0.6 dynamic_slice.29
  149.6 0.1 multiply_bitcast_fusion.1
  149.7 0.7 compare_bitcast_fusion
  150.4 0.6 dynamic_slice.31
  151.7 0.1 convert_element_type.47
  151.9 0.0 collective-permute-done
  151.9 0.0 collective-permute-done.2
  151.9 2.6 %fusion.19 = f32[3,512,1536]{2,1,0:T(8,128)S(1)} fusion(bf16[768,3,128]{2,0,1:T(8,128)(2,1)} %collective-permute-done.2, bf16[768,3,128]{2,0,1:T(8,128)(2,1)S(1)} %multiply_convert_fusion, f32[512,3,128]{0,2,1:T(8,128)S(1)} %get-tuple-element.20, f32[128]{0:T(128)S(1)} %copy-done.3, f32[512,3]{0,1:T(4,128)S(1)} %add_rsqrt_fusion.1), kind=kOutput, calls=%fused_computation.30 | convolution fusion | flops 606928896 | bytes 11409920 | tf_op jit(solution)/shard_map/qhd,khd->hqk/dot_general | solution.py:348
  154.5 5.4 %fusion.33 = (f32[3,512]{1,0:T(4,128)S(1)}, f32[3,512,1536]{2,1,0:T(8,128)}) fusion(f32[3,512,1536]{2,1,0:T(8,128)S(1)} %fusion.19, pred[1536]{0:T(1024)(128)(4,1)S(1)} %pad_add_fusion), kind=kOutput, calls=%fused_computation.68 | output fusion | flops 14157311 | bytes 18882048 | tf_op jit(solution)/shard_map/sub | solution.py:353
  159.9 5.7 %fusion.15 = bf16[3,128,512]{2,1,0:T(8,128)(2,1)S(1)} fusion(f32[3,512,1536]{2,1,0:T(8,128)} %get-tuple-element.22, f32[3,512]{1,0:T(4,128)S(1)} %get-tuple-element.21, bf16[768,3,128]{2,0,1:T(8,128)(2,1)} %collective-permute-done.1, bf16[768,3,128]{2,0,1:T(8,128)(2,1)S(1)} %fusion.26), kind=kOutput, calls=%fused_computation.24 | convolution fusion | flops 611254272 | bytes 11016192 | tf_op jit(solution)/shard_map/hqk,khd->qhd/dot_general | solution.py:355
  165.6 0.9 copy.20.attended
  166.5 26.5 %shard_map.114 = bf16[2,512,1536]{2,1,0:T(8,128)(2,1)} custom-call(bf16[512,384]{1,0:T(8,128)(2,1)} %copy.20.attended), custom_call_target="tpu_custom_call" | custom-call | tf_op jit(solution)/shard_map/pallas_call | solution.py:293
  193.0 4.0 %add_convert_fusion = bf16[2,512,384]{2,1,0:T(8,128)(2,1)S(1)} fusion(f32[2,384]{1,0:T(2,128)S(1)} %maximum_select_fusion, f32[512,384]{1,0:T(8,128)S(1)} %convert_element_type.47, bf16[2,512,1536]{2,1,0:T(8,128)(2,1)} %shard_map.114, bf16[1,1536,384]{2,1,0:T(8,128)(2,1)} %get-tuple-element.9), kind=kOutput, calls=%fused_computation.23 | convolution fusion | flops 1209139200 | bytes 5901312 | tf_op jit(solution)/shard_map/dot_general | solution.py:359
  197.0 1.3 multiply_add_fusion
  (28 shorter events, 0.1 us)
Async XLA Ops:
  1.5 150.3 %collective-permute-start = (f32[384]{0:T(512)S(1)}, f32[384]{0:T(512)S(1)}, u32[]{:S(2)}, u32[]{:S(2)}) collective-permute-start(f32[384]{0:T(512)S(1)} %get-tuple-element.16), channel_id=1, source_target_pairs={{0,16},{16,0},{1,17},{17,1},{2,18},{18,2},{3,19},{19,3},{4,20},{20... | collective-permute-start | bytes 4616 | tf_op jit(solution)/shard_map/ppermute | solution.py:26
  131.6 3.8 %copy-start = (bf16[768,3072]{1,0:T(8,128)(2,1)S(1)}, bf16[768,3072]{1,0:T(8,128)(2,1)}, u32[]{:S(2)}) copy-start(bf16[768,3072]{1,0:T(8,128)(2,1)} %get-tuple-element.7) | copy-start | bytes 14155780
  135.4 4.0 %slice-start = ((s8[7077888]{0:T(1024)(128)(4,1)}), s8[4194304]{0:T(1024)(128)(4,1)S(1)}, s32[]{:S(2)}) async-start(s8[7077888]{0:T(1024)(128)(4,1)} %bitcast.70), calls=%async_computation | async-start | bytes 8388608
  136.7 2.7 %slice-start.1 = ((s8[7077888]{0:T(1024)(128)(4,1)}), s8[2883584]{0:T(1024)(128)(4,1)S(1)}, s32[]{:S(2)}) async-start(s8[7077888]{0:T(1024)(128)(4,1)} %bitcast.70), calls=%async_computation.1 | async-start | bytes 5767168
  139.4 3.9 %copy-start.1 = (bf16[768,3072]{1,0:T(8,128)(2,1)}, bf16[768,3072]{1,0:T(8,128)(2,1)S(1)}, u32[]{:S(2)}) copy-start(bf16[768,3072]{1,0:T(8,128)(2,1)S(1)} %fusion.6) | copy-start | bytes 14155780
  139.4 4.5 %copy-start.5 = (f32[128]{0:T(128)S(1)}, f32[128]{0:T(128)}, u32[]{:S(2)}) copy-start(f32[128]{0:T(128)} %param.15) | copy-start | bytes 1540
  143.4 16.5 %collective-permute-start.1 = (bf16[768,3,128]{2,0,1:T(8,128)(2,1)S(1)}, bf16[768,3,128]{2,0,1:T(8,128)(2,1)}, u32[]{:S(2)}, u32[]{:S(2)}) collective-permute-start(bf16[768,3,128]{2,0,1:T(8,128)(2,1)S(1)} %fusion.26), channel_id=1, source_target_pairs={{0,1},{1,0},{2,3},{3,2},{4,5},{5,4},{6,7},{7,6},{8,9},{9,8},{10,11... | collective-permute-start | bytes 1769480 | tf_op jit(solution)/shard_map/ppermute | solution.py:26
  144.3 7.6 %collective-permute-start.2 = (bf16[768,3,128]{2,0,1:T(8,128)(2,1)S(1)}, bf16[768,3,128]{2,0,1:T(8,128)(2,1)}, u32[]{:S(2)}, u32[]{:S(2)}) collective-permute-start(bf16[768,3,128]{2,0,1:T(8,128)(2,1)S(1)} %multiply_convert_fusion), channel_id=1, source_target_pairs={{0,1},{1,0},{2,3},{3,2},{4,5},{5,4},{6,7},{7,6},{8,9},{9,8},{10,11... | collective-permute-start | bytes 1769480 | tf_op jit(solution)/shard_map/ppermute | solution.py:26
  144.8 4.1 %copy-start.6 = (s32[2,2]{1,0:T(2,128)S(1)}, s32[2,2]{1,0:T(2,128)}, u32[]{:S(2)}) copy-start(s32[2,2]{1,0:T(2,128)} %param.17) | copy-start | bytes 52
  144.8 4.7 %copy-start.4 = (s32[2,2,4]{2,1,0:T(2,128)S(1)}, s32[2,2,4]{2,1,0:T(2,128)}, u32[]{:S(2)}) copy-start(s32[2,2,4]{2,1,0:T(2,128)} %param.18) | copy-start | bytes 196
  144.8 5.6 %copy-start.7 = (s32[2]{0:T(128)S(1)}, s32[2]{0:T(128)}, u32[]{:S(2)}) copy-start(s32[2]{0:T(128)} %param.19) | copy-start | bytes 28
  144.8 6.8 %copy-start.2 = (bf16[512,384]{1,0:T(8,128)(2,1)S(1)}, bf16[512,384]{1,0:T(8,128)(2,1)}, u32[]{:S(2)}) copy-start(bf16[512,384]{1,0:T(8,128)(2,1)} %get-tuple-element.6) | copy-start | bytes 1179652
  144.8 7.1 %copy-start.3 = (f32[128]{0:T(128)S(1)}, f32[128]{0:T(128)}, u32[]{:S(2)}) copy-start(f32[128]{0:T(128)} %param.14) | copy-start | bytes 1540

commit v2 on v1

--- a/solution.py
+++ b/solution.py
@@ -44,6 +44,7 @@
 
 
 MESH = pl.DeviceIdType.MESH
+TEXT = 2
 
 
 class Sender:
@@ -87,9 +88,9 @@
 
 
 def gather_kernel(
-    n, tps, image, text, wqkv, wproj, acts, wfull, wcols, iblock,
-    act_send, act_recv, fwd_send, z_send, z_recv, x_send, x_recv, k_send, k_recv, kx_send, kx_recv,
-    own_send, own_recv, p_send, p_recv, i_send, i_recv,
+    n, tps, image, text, wqkv, wproj, mods, gains, queries, keys, values, wcols, iblock,
+    acts, wfull, normed, total, stage, act_send, act_recv, near_send, ix_send, fwd_send, z_send, z_recv, x_send, x_recv, k_send, k_recv, kx_send, kx_recv,
+    own_send, own_recv, st_send, st_recv, p_send, p_recv, i_send, i_recv,
 ):
     c, s, t = lax.axis_index("cfg"), lax.axis_index("seq"), lax.axis_index("tp")
     w, k, y = s % 2, t % 2, t // 2
@@ -108,6 +109,30 @@
     out = Sender()
     is_main = k == w
 
+    hrows = img // 2
+    ys = tps // 2
+
+    def act_part(block, part):
+        cols = pl.ds(pl.multiple_of(block * feats, 128), feats)
+        if part is TEXT:
+            return acts.at[pl.ds(img, txt), cols]
+        return acts.at[pl.ds(pl.multiple_of(part * hrows, 16), hrows), cols]
+
+    def act_source(part):
+        return text.at[0] if part is TEXT else image.at[pl.ds(pl.multiple_of(part * hrows, 16), hrows)]
+
+    for part in (TEXT, c):
+        dst = act_part(t, part)
+        index = 1 if part is TEXT else 0
+        src = act_source(part)
+        out.push(src, dst, act_send.at[ys, index], act_recv.at[t, part], (c, other_s, 2 * y + w))
+        for dy in range(1, ys):
+            to_y = (y + dy) % ys
+            out.push(src, dst, act_send.at[dy, index], act_recv.at[t, part], (c, s, 2 * to_y + w))
+    for part in (0, 1, TEXT):
+        src, dst = act_source(part), act_part(t, part)
+        out.push(src, dst, near_send.at[part], act_recv.at[t, part], (c, s, other_k), when=k != w)
+        guarded(k == w, pltpu.make_async_copy(src, dst, act_recv.at[t, part]).start)
     def rows_of(block, part, j):
         return pl.ds(pl.multiple_of(block * depth + part * half + j * chunk, 16), chunk)
 
@@ -119,41 +144,19 @@
                 wfull.at[rows_of(s, c, j)],
                 z_send.at[d, j], z_recv.at[d, j], (c, to, t), when=(to % 2) == k,
             )
-    def act_parts(block):
-        cols = pl.ds(pl.multiple_of(block * feats, 128), feats)
-        return [(0, acts.at[pl.ds(0, img), cols]), (1, acts.at[pl.ds(img, txt), cols])]
-
-    sources = [image, text.at[0]]
-    for part, dst in act_parts(t):
-        out.push(sources[part], dst, act_send.at[tps // 2, part], act_recv.at[t, part], (c, other_s, 2 * y + w))
-        for dy in range(1, tps // 2):
-            to_y = (y + dy) % (tps // 2)
-            out.push(sources[part], dst, act_send.at[dy, part], act_recv.at[t, part], (c, s, 2 * to_y + w))
-        out.push(sources[part], dst, act_send.at[0, part], act_recv.at[t, part], (c, s, other_k), when=k != w)
-        out.local(sources[part], dst, act_recv.at[t, part], when=k == w)
     own_rows = wfull.at[pl.ds(pl.multiple_of(s * depth, 16), depth)]
-    out.local(wqkv, own_rows, own_recv, when=is_main)
+    own_copy = pltpu.make_async_copy(wqkv, own_rows, own_recv)
+    guarded(is_main, own_copy.start)
     out.push(wqkv, own_rows, own_send, own_recv, (c, s, other_k), when=is_main)
     rows, width = wproj.shape
     pieces, _, piece = wcols.shape
     per = width // piece
-    total_half = (n * width) // 2
-    mine = (s * width) // total_half == c
-    first = (s * width - c * total_half) // piece
-    for h in range(per):
-        index = jnp.maximum(first + h, 0)
-        to_t = (index // pieces) % tps
-        slot = index % pieces
-        for ds in range(n):
-            to_s = (s + ds) % n
-            dst = wcols.at[slot, pl.ds(pl.multiple_of(t * rows, 16), rows)]
-            src = wproj.at[:, pl.ds(h * piece, piece)] if per > 1 else wproj
-            if ds == 0:
-                same = to_t == t
-                out.push(src, dst, p_send.at[ds, h], p_recv.at[slot, t], (c, to_s, to_t), when=mine & (to_t != t))
-                out.local(src, dst, p_recv.at[slot, t], when=mine & same)
-            else:
-                out.push(src, dst, p_send.at[ds, h], p_recv.at[slot, t], (c, to_s, to_t), when=mine)
+    groups = n // 2
+    mine = s // groups == c
+    spot = s % groups
+    guarded(mine, pltpu.make_async_copy(wproj, stage.at[spot], st_recv.at[0]).start)
+    for ds in range(1, n):
+        out.push(wproj, stage.at[spot], st_send.at[ds], st_recv.at[ds], (c, (s + ds) % n, t), when=mine)
     block = iblock.shape[1]
     for h in range(2):
         index = 2 * t + h
@@ -165,13 +168,26 @@
     far = k != w
     for dk in range(2):
         block_t = 2 * y + dk
-        for part, dst in act_parts(block_t):
+        for part in (TEXT, c):
+            index = 1 if part is TEXT else 0
+            dst = act_part(block_t, part)
             arrive(dst, act_recv.at[block_t, part], when=far)
-            for dy in range(1, tps // 2):
-                to_y = (y + dy) % (tps // 2)
+            for dy in range(1, ys):
+                to_y = (y + dy) % ys
                 out.push(
-                    dst, dst, fwd_send.at[dk, dy, part], act_recv.at[block_t, part], (c, s, 2 * to_y + k), when=far
+                    dst, dst, fwd_send.at[dk, dy, index], act_recv.at[block_t, part], (c, s, 2 * to_y + k), when=far
                 )
+            if part is not TEXT:
+                out.push(dst, dst, ix_send.at[dk], act_recv.at[block_t, part], (1 - c, s, t), when=far)
+
+    def swap_images():
+        for dy in range(1, ys):
+            for dk in range(2):
+                block_t = 2 * ((y + dy) % ys) + dk
+                dst = act_part(block_t, c)
+                arrive(dst, act_recv.at[block_t, c])
+                out.push(dst, dst, ix_send.at[2 * dy + dk], act_recv.at[block_t, c], (1 - c, s, t))
+
     for d in range(1, n):
         origin = (s - d + n) % n
         for j in range(chunks):
@@ -179,35 +195,78 @@
             arrive(dst, z_recv.at[d, j], when=is_main)
             out.push(dst, dst, x_send.at[d, j], x_recv.at[d, j], (1 - c, s, t), when=is_main)
             out.push(dst, dst, k_send.at[d, j], k_recv.at[d, j], (c, s, other_k), when=is_main)
+        if d == 1:
+            swap_images()
+    for block_t in range(tps):
+        here = block_t // 2 == y
+        for part in (0, 1, TEXT):
+            done = (here & far & ((part is TEXT) | (c == part))) | (~here & (c == part))
+            arrive(act_part(block_t, part), act_recv.at[block_t, part], when=~done)
+    fan = 32
+
+    @pl.loop(0, (img + txt) // fan)
+    def _(step):
+        at = pl.ds(pl.multiple_of(step * fan, fan), fan)
+        rows_in = acts[at].astype(jnp.float32)
+        normed[at] = ((1.0 + mods[1:2]) * layer_norm(rows_in) + mods[0:1]).astype(jnp.bfloat16)
+
+    wide = wfull.shape[1] // 3
+    band = (img + txt) // 3
+
+    def multiply(start, size, fresh):
+        at_k = pl.ds(pl.multiple_of(start, 128), size)
+
+        @pl.loop(0, 3)
+        def _(step):
+            at = pl.ds(pl.multiple_of(step * band, 16), band)
+            for third in range(3):
+                at_c = pl.ds(third * wide, wide)
+                product = jnp.dot(normed[at, at_k], wfull[at_k, at_c], preferred_element_type=jnp.float32)
+                total[at, at_c] = product if fresh else total[at, at_c] + product
+
+    by_block = depth % 128 == 0
+    arrive(own_rows, own_recv, when=~is_main)
+    guarded(is_main, own_copy.wait)
+    if by_block:
+        multiply(s * depth, depth, True)
+    for group in range(groups):
+        origin = c * groups + group
+        for ds in range(n):
+            arrive(stage.at[group], st_recv.at[ds], when=(s - origin + n) % n == ds)
+        for h in range(per):
+            to_t = (group * per + h) // pieces
+            slot = (group * per + h) % pieces
+            src = stage.at[group, :, pl.ds(h * piece, piece)] if per > 1 else stage.at[group]
+            dst = wcols.at[slot, pl.ds(pl.multiple_of(t * rows, 16), rows)]
+            out.push(src, dst, p_send.at[group, h], p_recv.at[slot, t], (c, s, to_t), when=to_t != t)
+            out.local(src, dst, p_recv.at[slot, t], when=to_t == t)
     for d in range(1, n):
         origin = (s - d + n) % n
         for j in range(chunks):
             dst = wfull.at[rows_of(origin, 1 - c, j)]
             arrive(dst, x_recv.at[d, j], when=is_main)
             out.push(dst, dst, kx_send.at[d, j], kx_recv.at[d, j], (c, s, other_k), when=is_main)
-    for d in range(1, n):
-        origin = (s - d + n) % n
         for j in range(chunks):
             arrive(wfull.at[rows_of(origin, c, j)], k_recv.at[d, j], when=~is_main)
             arrive(wfull.at[rows_of(origin, 1 - c, j)], kx_recv.at[d, j], when=~is_main)
-    arrive(own_rows, own_recv, when=~is_main)
-    for block_t in range(tps):
-        for part, dst in act_parts(block_t):
-            waited = far & (block_t // 2 == y)
-            own = (k == w) & (block_t == t)
-            arrive(dst, act_recv.at[block_t, part], when=~(waited | own))
-    needed_first = t * pieces
+        if by_block:
+            multiply(origin * depth, depth, False)
+    if not by_block:
+        multiply(0, n * depth, True)
+    for head in range(wfull.shape[1] // (3 * HD)):
+        at_h = pl.ds(head * HD, HD)
+        queries[:, at_h] = head_norm(total[pl.ds(0, img), pl.ds(head * 3 * HD, HD)], gains[0:1])
+        keys[:, at_h] = head_norm(total[:, pl.ds(head * 3 * HD + HD, HD)], gains[1:2])
+        values[:, at_h] = total[:, pl.ds(head * 3 * HD + 2 * HD, HD)].astype(jnp.bfloat16)
     for slot in range(pieces):
-        own_source = ((c * total_half + t * pieces * piece + slot * piece) // width) == s
         for from_t in range(tps):
-            dst = wcols.at[slot, pl.ds(from_t * rows, rows)]
-            arrive(dst, p_recv.at[slot, from_t], when=~(own_source & (from_t == t)))
+            arrive(wcols.at[slot, pl.ds(from_t * rows, rows)], p_recv.at[slot, from_t], when=t != from_t)
     own_image = (c * tps + t) // 2 == t
     arrive(iblock, i_recv, when=~own_image)
     out.finish()
 
 
-def gather_all(n, tps, image, text, wqkv, wproj):
+def gather_all(n, tps, image, text, wqkv, wproj, mods, gains):
     img, feats = image.shape
     txt = text.shape[1]
     depth, cols = wqkv.shape
@@ -220,25 +279,32 @@
     per = width // piece
     dma = pltpu.SemaphoreType.DMA
     any_space = pl.BlockSpec(memory_space=pl.ANY)
+    vmem = pl.BlockSpec(memory_space=pltpu.VMEM)
     bf16 = jnp.bfloat16
     return pl.pallas_call(
         functools.partial(gather_kernel, n, tps),
         out_shape=(
-            jax.ShapeDtypeStruct((img + txt, tps * feats), bf16),
-            jax.ShapeDtypeStruct((n * depth, cols), bf16),
+            jax.ShapeDtypeStruct((img, cols // 3), bf16),
+            jax.ShapeDtypeStruct((img + txt, cols // 3), bf16),
+            jax.ShapeDtypeStruct((img + txt, cols // 3), bf16),
             jax.ShapeDtypeStruct((pieces, tps * rows, piece), bf16),
             jax.ShapeDtypeStruct((img, block), bf16),
         ),
-        in_specs=[any_space] * 4,
-        out_specs=(any_space,) * 4,
+        in_specs=[any_space] * 4 + [vmem] * 2,
+        out_specs=(vmem,) * 3 + (any_space,) * 2,
         scratch_shapes=[
-            dma((tps // 2 + 1, 2)), dma((tps, 2)), dma((2, tps // 2, 2)),
+            pltpu.VMEM((img + txt, tps * feats), bf16),
+            pltpu.VMEM((n * depth, cols), bf16),
+            pltpu.VMEM((img + txt, tps * feats), bf16),
+            pltpu.VMEM((img + txt, cols), jnp.float32),
+            pltpu.VMEM((n // 2, rows, width), bf16),
+            dma((tps // 2 + 1, 2)), dma((tps, 3)), dma((3,)), dma((tps,)), dma((2, tps // 2, 2)),
             dma((n, chunks)), dma((n, chunks)), dma((n, chunks)), dma((n, chunks)),
             dma((n, chunks)), dma((n, chunks)), dma((n, chunks)), dma((n, chunks)),
-            dma, dma, dma((n, per)), dma((pieces, tps)), dma((2,)), dma,
+            dma, dma, dma((n,)), dma((n,)), dma((n // 2, per)), dma((pieces, tps)), dma((2,)), dma,
         ],
-        compiler_params=pltpu.CompilerParams(collective_id=0, has_side_effects=True),
-    )(image, text, wqkv, wproj)
+        compiler_params=pltpu.CompilerParams(collective_id=0, has_side_effects=True, vmem_limit_bytes=48 * 1024 * 1024),
+    )(image, text, wqkv, wproj, mods, gains)
 
 
 def exchange_kernel(n, tps, attended, gathered, send, recv, fwd_send, fwd_recv):
@@ -315,21 +381,15 @@
     gate_own = lax.dynamic_index_in_dim(gate_rows, cfg_pos * tp_count + tp_pos, 0, keepdims=False)
     gate_sent = lax.dynamic_index_in_dim(gate_rows, (1 - cfg_pos) * tp_count + tp_pos, 0, keepdims=False)
     gate_far = from_partner(gate_sent, "cfg", 0)
-    acts, piece, wcols, image_block = gather_all(seq_count, tp_count, image, text, w_qkv, w_proj)
+    query, keys_own, values_own, wcols, image_block = gather_all(
+        seq_count, tp_count, image, text, w_qkv, w_proj, mods[:2], jnp.stack([q_gain, k_gain])
+    )
     img_rows = image.shape[0]
     txt_rows = text.shape[1]
-    normed = ((1.0 + mods[1]) * layer_norm(acts.astype(jnp.float32)) + mods[0]).astype(jnp.bfloat16)
     heads_dev = w_qkv.shape[1] // (3 * HD)
-    count = piece.shape[0]
-    blocks = piece.reshape(count, heads_dev, 3, HD)
-    query_weight = blocks[:, :, 0].reshape(count, heads_dev * HD)
-    pair_weight = blocks[:, :, 1:].reshape(count, heads_dev * 2 * HD)
-    query_sum = jnp.dot(normed[:img_rows], query_weight, preferred_element_type=jnp.float32)
-    pair_sum = jnp.dot(normed, pair_weight, preferred_element_type=jnp.float32)
-    query = head_norm(query_sum.reshape(img_rows, heads_dev, HD), q_gain)
-    pairs = pair_sum.reshape(-1, heads_dev, 2, HD)
-    keys_own = head_norm(pairs[:, :, 0], k_gain)
-    values_own = pairs[:, :, 1].astype(jnp.bfloat16)
+    query = query.reshape(img_rows, heads_dev, HD)
+    keys_own = keys_own.reshape(-1, heads_dev, HD)
+    values_own = values_own.reshape(-1, heads_dev, HD)
     keys_far, values_far = from_partner((keys_own, values_own), "tp", 0)
     length_now = lax.dynamic_slice(text_len, (cfg_pos, prompt), (1, 1))[0, 0]
     order_row = lax.dynamic_slice(text_tiles, (cfg_pos, prompt, 0), (1, 1, 4))[0, 0]

time: 199 us -> 173 us (0.87)
  matrix products: 20.2 us -> 11.8 us
  other arithmetic: 16.4 us -> 9 us
  Pallas kernels: 143 us -> 136 us
  local copies, waits for them, and re-layouts: 13.1 us -> 10 us
    pallas_call x1, Pallas kernels: 117 us -> 95.5 us  [gather_all(): pl.pallas_call(functools.partial(gather_kernel, n, tps), out_shape=(jax.S...]
    pallas_call x1, Pallas kernels: 26.5 us -> 40.4 us  [exchange(): pl.pallas_call(functools.partial(exchange_kernel, n, tps), out_shape=jax....]
    dot_general x2 -> x0, matrix products: 7.94 us -> none  [the longest x1 4.09 us: local(): jnp.dot(normed[:img_rows], query_weight, preferred_element_type=jnp.float32)]
    pallas_call x1 -> x3, local copies, waits for them, and re-layouts: 10.3 us -> 2.36 us  [gather_all(): pl.pallas_call(functools.partial(gather_kernel, n, tps), out_shape=(jax.S...]
    reduce_sum x3 -> x0, other arithmetic: 4.91 us -> none  [the longest x1 3.17 us: layer_norm(): mean_value = jnp.mean(rows, axis=-1, keepdims=True)]
    unnamed x20, local copies, waits for them, and re-layouts: 0.61 us -> 4.13 us
    convert_element_type x2 -> x0, other arithmetic: 3.01 us -> none  [the longest x1 2.63 us: local(): ((1.0 + mods[1]) * layer_norm(acts.astype(jnp.float32)) + mods[0]).astype...]
  transfers between devices with their start and end apart: 3 -> 3, of which waited for: 0 -> 0; matrix products, arithmetic and copies ran while one was open for 18% -> 7% of each run, Pallas kernels for 59% -> 0%
where the time goes in v2:
time: 173 us; the launch traced here: 172 us
  Pallas kernels  136 us (79%)
  matrix products  11.8 us (7%)
  local copies, waits for them, and re-layouts  10 us (6%)
  other arithmetic  9 us (5%)
  starting transfers between devices  3.88 us (2%)
    pallas_call x1, Pallas kernels, gather_all(): pl.pallas_call(functools.partial(gather_kernel, n, tps), out_shape=(jax.S...  95.5 us
    pallas_call x1, Pallas kernels, exchange(): pl.pallas_call(functools.partial(exchange_kernel, n, tps), out_shape=jax....  40.4 us
    dot_general x1, matrix products, local(): jnp.einsum('hqk,khd->qhd', probs, values_all, preferred_element_type=jnp....  5.65 us
    sub x1, other arithmetic, local(): exps = jnp.exp(scores - row_max)  5.22 us
    unnamed x20, local copies, waits for them, and re-layouts  4.13 us
    ppermute x3, starting transfers between devices, from_partner(): return lax.ppermute(block, axis, route)  3.88 us
    dot_general x1, matrix products, local(): jnp.dot(gathered.reshape(2 * img_rows, -1), weight, preferred_element_typ...  3.67 us
  transfers between devices with their start and end apart: 3, of which 0 were waited for; matrix products, arithmetic and copies ran while one was open for 7% of the time, Pallas kernels for 0%

profile of v2, /device:TPU:0, one launch (start us, length us, event | category | flops | bytes accessed | tf_op | source)
XLA Modules:
  0.0 172.2 jit_solution(4670381139409209998)
XLA Ops:
  0.6 0.0 copy-start
  0.7 0.9 copy-done
  1.6 0.7 pad_maximum_fusion.gains
  2.3 1.1 copy-done.1
  3.4 1.1 copy-done.2
  4.5 1.0 copy-done.3
  5.5 95.5 %shard_map.113 = (bf16[512,384]{1,0:T(8,128)(2,1)S(1)}, bf16[768,384]{1,0:T(8,128)(2,1)S(1)}, bf16[768,384]{1,0:T(8,128)(2,1)S(1)}, bf16[1,1536,384]{2,1,0:T(8,128)(2,1)S(1)}, bf16[512,384]{1,0:T(8,128)(2,1)S(1)}) custom-call(bf16[512,768]{1,0:T(8,128)(2,1)S(1)} %copy-done.1, bf16[1,256,768]{2,1,0:T(8,128)(2,1)S(1)} %copy-done.3, bf16[768,1152]{1,0:T(8,128)(2,1)} %wqkv.1, ...), custom_call_target="tpu_custom_call" | custom-call | tf_op jit(solution)/shard_map/pallas_call | solution.py:284
  101.0 1.1 copy.22
  102.1 1.4 copy.24
  103.5 1.9 %collective-permute-start.2 = (bf16[768,3,128]{2,0,1:T(8,128)(2,1)S(1)}, bf16[768,3,128]{2,0,1:T(8,128)(2,1)}, u32[]{:S(2)}, u32[]{:S(2)}) collective-permute-start(bf16[768,3,128]{2,0,1:T(8,128)(2,1)S(1)} %copy.24), channel_id=1, source_target_pairs={{0,1},{1,0},{2,3},{3,2},{4,5},{5,4},{6,7},{7,6},{8,9},{9,8},{10,11... | collective-permute-start | bytes 1769480 | tf_op jit(solution)/shard_map/ppermute | solution.py:26
  105.3 1.1 copy.20
  106.4 0.0 collective-permute-start.1
  106.5 2.0 %collective-permute-start = (f32[384]{0:T(512)S(1)}, f32[384]{0:T(512)S(1)}, u32[]{:S(2)}, u32[]{:S(2)}) collective-permute-start(f32[384]{0:T(512)S(1)} %get-tuple-element.15), channel_id=1, source_target_pairs={{0,16},{16,0},{1,17},{17,1},{2,18},{18,2},{3,19},{19,3},{4,20},{20... | collective-permute-start | bytes 4616 | tf_op jit(solution)/shard_map/ppermute | solution.py:26
  108.5 0.0 copy-done.7
  108.5 0.6 dynamic_slice.29
  109.1 0.1 multiply_bitcast_fusion.1
  109.2 0.7 compare_bitcast_fusion
  109.9 0.6 dynamic_slice.31
  111.2 0.2 copy.21
  111.4 0.9 convert_element_type.31
  112.4 0.0 collective-permute-done
  112.4 0.0 collective-permute-done.2
  112.5 2.5 %fusion.10 = f32[3,512,1536]{2,1,0:T(8,128)S(1)} fusion(bf16[512,3,128]{0,2,1:T(8,128)(2,1)S(1)} %bitcast.47, bf16[768,3,128]{2,0,1:T(8,128)(2,1)} %collective-permute-done.2, bf16[768,3,128]{2,0,1:T(8,128)(2,1)S(1)} %copy.24), kind=kOutput, calls=%fused_computation.14 | convolution fusion | flops 606339072 | bytes 11010048 | tf_op jit(solution)/shard_map/qhd,khd->hqk/dot_general | solution.py:408
  115.0 0.0 copy-start.5
  115.0 5.2 %fusion.22 = (f32[3,512]{1,0:T(4,128)S(1)}, f32[3,512,1536]{2,1,0:T(8,128)}) fusion(f32[3,512,1536]{2,1,0:T(8,128)S(1)} %fusion.10, pred[1536]{0:T(1024)(128)(4,1)S(1)} %pad_add_fusion), kind=kOutput, calls=%fused_computation.43 | output fusion | flops 14157311 | bytes 18882048 | tf_op jit(solution)/shard_map/sub | solution.py:413
  120.2 0.0 collective-permute-done.1
  120.2 5.6 %fusion.6 = bf16[3,128,512]{2,1,0:T(8,128)(2,1)S(1)} fusion(f32[3,512,1536]{2,1,0:T(8,128)} %get-tuple-element.19, f32[3,512]{1,0:T(4,128)S(1)} %get-tuple-element.18, bf16[768,3,128]{0,2,1:T(8,128)(2,1)} %collective-permute-done.1, bf16[768,3,128]{0,2,1:T(8,128)(2,1)S(1)} %bitcast.49), kind=kOutput, calls=%fused_computation.10 | convolution fusion | flops 611254272 | bytes 11016192 | tf_op jit(solution)/shard_map/hqk,khd->qhd/dot_general | solution.py:415
  125.9 0.0 copy-start.4
  125.9 0.9 copy.26.attended
  126.8 40.4 %shard_map.114 = bf16[2,512,1536]{2,1,0:T(8,128)(2,1)} custom-call(bf16[512,384]{1,0:T(8,128)(2,1)} %copy.26.attended), custom_call_target="tpu_custom_call" | custom-call | tf_op jit(solution)/shard_map/pallas_call | solution.py:359
  167.2 3.7 %add_convert_fusion = bf16[2,512,384]{2,1,0:T(8,128)(2,1)S(1)} fusion(f32[2,384]{1,0:T(2,128)S(1)} %maximum_select_fusion, f32[512,384]{1,0:T(8,128)S(1)} %copy-done.4, bf16[2,512,1536]{2,1,0:T(8,128)(2,1)} %shard_map.114, bf16[1,1536,384]{2,1,0:T(8,128)(2,1)S(1)} %get-tuple-element.11), kind=kOutput, calls=%fused_computation.9 | convolution fusion | flops 1209139200 | bytes 5901312 | tf_op jit(solution)/shard_map/dot_general | solution.py:419
  170.9 1.3 multiply_add_fusion
  (19 shorter events, 0.2 us)
Async XLA Ops:
  0.6 0.9 copy-start
  2.3 1.1 copy-start.1
  3.4 1.1 copy-start.2
  4.5 1.0 copy-start.3
  5.4 103.1 %copy-start.7 = (s32[2,2]{1,0:T(2,128)S(1)}, s32[2,2]{1,0:T(2,128)}, u32[]{:S(2)}) copy-start(s32[2,2]{1,0:T(2,128)} %param.17) | copy-start | bytes 52
  5.4 103.6 %copy-start.6 = (s32[2,2,4]{2,1,0:T(2,128)S(1)}, s32[2,2,4]{2,1,0:T(2,128)}, u32[]{:S(2)}) copy-start(s32[2,2,4]{2,1,0:T(2,128)} %param.18) | copy-start | bytes 196
  5.5 104.5 %copy-start.8 = (s32[2]{0:T(128)S(1)}, s32[2]{0:T(128)}, u32[]{:S(2)}) copy-start(s32[2]{0:T(128)} %param.19) | copy-start | bytes 28
  103.5 9.0 %collective-permute-start.2 = (bf16[768,3,128]{2,0,1:T(8,128)(2,1)S(1)}, bf16[768,3,128]{2,0,1:T(8,128)(2,1)}, u32[]{:S(2)}, u32[]{:S(2)}) collective-permute-start(bf16[768,3,128]{2,0,1:T(8,128)(2,1)S(1)} %copy.24), channel_id=1, source_target_pairs={{0,1},{1,0},{2,3},{3,2},{4,5},{5,4},{6,7},{7,6},{8,9},{9,8},{10,11... | collective-permute-start | bytes 1769480 | tf_op jit(solution)/shard_map/ppermute | solution.py:26
  106.4 13.8 %collective-permute-start.1 = (bf16[768,3,128]{0,2,1:T(8,128)(2,1)}, bf16[768,3,128]{0,2,1:T(8,128)(2,1)}, u32[]{:S(2)}, u32[]{:S(2)}) collective-permute-start(bf16[768,3,128]{0,2,1:T(8,128)(2,1)} %bitcast.48), channel_id=1, source_target_pairs={{0,1},{1,0},{2,3},{3,2},{4,5},{5,4},{6,7},{7,6},{8,9},{9,8},{10,11... | collective-permute-start | bytes 1769480 | tf_op jit(solution)/shard_map/ppermute | solution.py:26
  106.5 5.9 %collective-permute-start = (f32[384]{0:T(512)S(1)}, f32[384]{0:T(512)S(1)}, u32[]{:S(2)}, u32[]{:S(2)}) collective-permute-start(f32[384]{0:T(512)S(1)} %get-tuple-element.15), channel_id=1, source_target_pairs={{0,16},{16,0},{1,17},{17,1},{2,18},{18,2},{3,19},{19,3},{4,20},{20... | collective-permute-start | bytes 4616 | tf_op jit(solution)/shard_map/ppermute | solution.py:26
  115.0 5.2 %copy-start.5 = (bf16[768,384]{0,1:T(8,128)(2,1)S(1)}, bf16[768,384]{0,1:T(8,128)(2,1)}, u32[]{:S(2)}) copy-start(bf16[768,384]{0,1:T(8,128)(2,1)} %copy.20) | copy-start | bytes 1769476
  125.9 41.3 %copy-start.4 = (f32[512,384]{1,0:T(8,128)S(1)}, f32[512,384]{1,0:T(8,128)}, u32[]{:S(2)}) copy-start(f32[512,384]{1,0:T(8,128)} %convert_element_type.31) | copy-start | bytes 2359300
